TPU v7x, 256 devices: a whole 4x4x8 slice. The times are simulated.
256 devices in a mesh: row: 8 (over y, core), col: 32 (over x, z).
Axes of the slice: x: 4, y: 4, z: 8, core: 2. Of those that a mesh axis runs over, the one named last changes fastest.
Arguments:
- tokens: bfloat16 [1024, 8192], P('col', 'row'), may hold values from -6 to 6
- gate_weight: bfloat16 [8192, 28672], P('row', 'col'), may hold values from -0.0625 to 0.0625
- up_weight: bfloat16 [8192, 28672], P('row', 'col'), may hold values from -0.0625 to 0.0625
- down_weight: bfloat16 [28672, 8192], P('col', 'row'), may hold values from -0.03125 to 0.03125
- out_grad: bfloat16 [1024, 8192], P('col', 'row'), may hold values from -0.1875 to 0.1875
Outputs:
- mixed: bfloat16 [1024, 8192], P('col', 'row')
- down_grad: float32 [28672, 8192], P('col', 'row')
All inputs are finite; a program needn't handle non-finite values.
Results may differ from a plain program's by a relative error of at most 0.0049.
Values may be sent and summed in bfloat16 or wider, within the bound.
A program may use at most 64 MiB of HBM per device.

v0:
```python
import jax
import jax.numpy as jnp
from jax import lax
from jax.sharding import PartitionSpec as P


def local(tokens, gate_weight, up_weight, down_weight, out_grad):
    hidden_width = gate_weight.shape[1]
    piece = lax.all_gather(tokens, "col", axis=0, tiled=True)
    gate_part = jnp.dot(piece, gate_weight, preferred_element_type=jnp.float32)
    up_part = jnp.dot(piece, up_weight, preferred_element_type=jnp.float32)
    partial_sums = jnp.concatenate([gate_part, up_part], axis=1)
    summed = lax.psum(partial_sums, "row")
    hidden = (jax.nn.silu(summed[:, :hidden_width]) * summed[:, hidden_width:]).astype(jnp.bfloat16)
    block = hidden
    mixed = lax.psum_scatter(
        jnp.dot(block, down_weight, preferred_element_type=jnp.float32),
        "col",
        scatter_dimension=0,
        tiled=True,
    ).astype(jnp.bfloat16)
    block = hidden
    down_grad = lax.dot_general(
        block,
        lax.all_gather(out_grad, "col", axis=0, tiled=True),
        (((0,), (0,)), ((), ())),
        preferred_element_type=jnp.float32,
    )
    return (mixed, down_grad)


def solution(mesh):
    return jax.shard_map(
        local,
        mesh=mesh,
        in_specs=(
            P("col", "row"),
            P("row", "col"),
            P("row", "col"),
            P("col", "row"),
            P("col", "row"),
        ),
        out_specs=(P("col", "row"), P("col", "row")),
        check_vma=False,
    )
```

profile of v0, /device:TPU:1, one launch (start us, length us, event | category | flops | bytes accessed | tf_op | source)
XLA Modules:
  0.0 504.7 jit_solution(5885085214703608429)
XLA Ops:
  7.2 0.0 copy-start
  7.2 0.0 all-gather.3.cloned.1.call-start
  7.2 0.7 all-gather.3.cloned.1.call-update
  7.9 0.0 all-reduce.2.cloned.1.call-start
  8.0 80.5 %all-gather.3.cloned.1.call-done = bf16[1024,1024]{1,0:T(8,128)(2,1)} async-done(((bf16[32,1024]{1,0:T(8,128)(2,1)}), bf16[1024,1024]{1,0:T(8,128)(2,1)}) %all-gather.3.cloned.1.call-update) | async-done | bytes 2097168 | tf_op jit(solution)/shard_map/all_gather | solution.py:9
  88.4 4.5 fusion.1
  92.9 0.0 copy-done.2
  92.9 0.0 copy-done.3
  92.9 2.2 fusion.2
  95.1 3.7 pad_maximum_fusion
  98.8 0.0 all-reduce.2.cloned.1.call-update
  98.9 0.0 all-gather.5.cloned.1.call-start
  98.9 0.7 all-gather.5.cloned.1.call-update
  99.6 0.0 reduce-scatter.2.cloned.1.call-start
  99.6 99.3 %all-reduce.2.cloned.1.call-done = f32[1024,1792]{0,1:T(8,128)} async-done(((f32[1024,1792]{0,1:T(8,128)}), f32[1024,1792]{0,1:T(8,128)}) %all-reduce.2.cloned.1.call-update) | async-done | bytes 7340048 | tf_op jit(solution)/shard_map/psum | solution.py:13
  198.9 4.3 fusion
  203.3 0.0 copy-start.1
  203.3 1.3 copy-done.1
  204.5 4.4 fusion.3
  208.9 0.0 reduce-scatter.2.cloned.1.call-update
  208.9 66.8 %all-gather.5.cloned.1.call-done = bf16[1024,1024]{1,0:T(8,128)(2,1)} async-done(((bf16[32,1024]{1,0:T(8,128)(2,1)}), bf16[1024,1024]{1,0:T(8,128)(2,1)}) %all-gather.5.cloned.1.call-update) | async-done | bytes 2097168 | tf_op jit(solution)/shard_map/all_gather | solution.py:25
  275.7 6.0 %fusion.4 = f32[896,1024]{1,0:T(8,128)} fusion(bf16[1024,896]{0,1:T(8,128)(2,1)} %copy-done.1, bf16[1024,1024]{1,0:T(8,128)(2,1)} %all-gather.5.cloned.1.call-done), kind=kOutput, calls=%fused_computation.6 | convolution fusion | flops 1879048192 | bytes 7602176 | tf_op jit(solution)/shard_map/dot_general | solution.py:23
  281.8 214.8 %reduce-scatter.2.cloned.1.call-done = f32[32,1024]{1,0:T(8,128)} async-done(((f32[1024,1024]{1,0:T(8,128)}), f32[32,1024]{1,0:T(8,128)}) %reduce-scatter.2.cloned.1.call-update) | async-done | bytes 131088 | tf_op jit(solution)/shard_map/reduce_scatter | solution.py:16
  496.6 1.5 convert_element_type.7
  (3 shorter events, 0.0 us)
Async XLA Ops:
  7.2 197.4 %copy-start = (bf16[896,1024]{1,0:T(8,128)(2,1)S(1)}, bf16[896,1024]{1,0:T(8,128)(2,1)}, u32[]{:S(2)}) copy-start(bf16[896,1024]{1,0:T(8,128)(2,1)} %param.8) | copy-start | bytes 5505028
  7.2 81.2 %all-gather.3.cloned.1.call-start = ((), (), s32[]{:S(2)}) async-start(), calls=%async_computation.1 | async-start | bytes 2162688 | tf_op jit(solution)/shard_map/all_gather | solution.py:9
  7.9 191.0 %all-reduce.2.cloned.1.call-start = ((), (), s32[]{:S(2)}) async-start(), calls=%async_computation.2 | async-start | bytes 14680064 | tf_op jit(solution)/shard_map/psum | solution.py:13
  88.4 4.5 copy-start.2
  88.4 4.5 copy-start.3
  98.9 176.9 %all-gather.5.cloned.1.call-start = ((), (), s32[]{:S(2)}) async-start(), calls=%async_computation.4 | async-start | bytes 2162688 | tf_op jit(solution)/shard_map/all_gather | solution.py:25
  99.6 397.0 %reduce-scatter.2.cloned.1.call-start = ((), (), s32[]{:S(2)}) async-start(), calls=%async_computation.3 | async-start | bytes 4325376 | tf_op jit(solution)/shard_map/reduce_scatter | solution.py:16
  203.3 1.3 copy-start.1
Sparse Core Ops, SparseCore 0:
  10.6 77.7 all-gather.2
  99.0 99.9 all-reduce.1
  201.5 74.1 all-gather.4
  279.5 217.0 reduce-scatter.1
where the time goes:
time: 509 us; the launch traced here: 505 us
  waiting for transfers between devices  463 us (91%)
  matrix products  17 us (3%)
  between operations  13.8 us (3%)
  other arithmetic  9.59 us (2%)
    reduce_scatter x1, waiting for transfers between devices, local(): lax.psum_scatter(jnp.dot(block, down_weight, preferred_element_type=jnp.f...  215 us
    psum x1, waiting for transfers between devices, local(): summed = lax.psum(partial_sums, 'row')  99.3 us
    all_gather x1, waiting for transfers between devices, local(): piece = lax.all_gather(tokens, 'col', axis=0, tiled=True)  80.5 us
    all_gather x1, waiting for transfers between devices, local(): lax.all_gather(out_grad, 'col', axis=0, tiled=True)  66.8 us
  transfers between devices with their start and end apart: 4, of which 4 were waited for; matrix products, arithmetic and copies ran while one was open for 3% of the time, Pallas kernels for 0%

commit v1 on v0

v1 whole, which is shorter than its diff:
```python
import jax
import jax.numpy as jnp
from jax import lax
from jax.experimental import pallas as pl
from jax.experimental.pallas import tpu as pltpu
from jax.sharding import PartitionSpec as P

MESH = pl.DeviceIdType.MESH
BF16, F32 = jnp.bfloat16, jnp.float32
NX, NY, NZ = 4, 4, 8
OWN = 32
CHUNK = NX * OWN
PART = CHUNK // (2 * NY)


def kernel(
    tokens, gate_w, up_w, down_w, out_grad, mixed, down_grad,
    w, wd, tok, og, part, core_in, y_out, y_in, hid, hid_t, x_own, x_out, x_in, z_out, z_in, dg,
    w_sem, dg_sem,
    zt_s, zt_r, xt_s, xt_r, c1_s, c1_r, y1_s, y1_r, y2_s, y2_r, c2_s, c2_r, x2_s, x2_r, z2_s, z2_r, ox_s, ox_r, oz_s, oz_r,
):
    ff = gate_w.shape[1]
    row, col = lax.axis_index("row"), lax.axis_index("col")
    y, c, x, z = row // 2, row % 2, col // NZ, col % NZ

    def dev(px, py, pz, pc):
        return (py * 2 + pc, px * NZ + pz)

    x_peer = [dev((x + j) % NX, y, z, c) for j in range(NX)]
    y_peer = [dev(x, (y + j) % NY, z, c) for j in range(NY)]
    z_up, z_down = dev(x, y, (z + 1) % NZ, c), dev(x, y, (z + NZ - 1) % NZ, c)
    sibling = dev(x, y, z, 1 - c)

    def send(src, dst, ss, rs, to):
        return pltpu.make_async_remote_copy(
            src_ref=src, dst_ref=dst, send_sem=ss, recv_sem=rs, device_id=to, device_id_type=MESH)

    def arrived(dst, ss, rs):
        send(dst, dst, ss, rs, sibling).wait_recv()

    def sent(src, ss, rs):
        send(src, src, ss, rs, sibling).wait_send()

    loads = [
        pltpu.make_async_copy(gate_w, w.at[:, pl.ds(0, ff)], w_sem.at[0]),
        pltpu.make_async_copy(up_w, w.at[:, pl.ds(ff, ff)], w_sem.at[1]),
        pltpu.make_async_copy(down_w, wd, w_sem.at[2]),
    ]
    for load in loads:
        load.start()

    barrier = pltpu.get_barrier_semaphore()
    for j in range(1, NX):
        pl.semaphore_signal(barrier, inc=1, device_id=x_peer[j], device_id_type=MESH)
    for j in range(1, NY):
        pl.semaphore_signal(barrier, inc=1, device_id=y_peer[j], device_id_type=MESH)
    for j in range(1, NZ):
        pl.semaphore_signal(barrier, inc=1, device_id=dev(x, y, (z + j) % NZ, c), device_id_type=MESH)
    pl.semaphore_signal(barrier, inc=1, device_id=sibling, device_id_type=MESH)
    tok[0, x] = tokens[...]
    og[0, x] = out_grad[...]
    pl.semaphore_wait(barrier, NX + NY + NZ - 2)

    def tok_x(r):
        for j in (2, 1, 3):
            send(tok.at[r, x], tok.at[r, x], xt_s.at[r, j - 1], xt_r.at[r, j - 1], x_peer[j]).start()

    def tok_step(d):
        half = OWN // 2
        if d == 0:
            send(tok.at[0, x], tok.at[NZ - 1, x], zt_s.at[NZ - 1], zt_r.at[NZ - 1], z_up).start()
            send(tok.at[0, x], tok.at[1, x], zt_s.at[1], zt_r.at[1], z_down).start()
            tok_x(0)
        elif d < NZ // 2:
            e = NZ - d
            arrived(tok.at[d, x], zt_s.at[d], zt_r.at[d])
            if d < NZ // 2 - 1:
                send(tok.at[d, x], tok.at[d + 1, x], zt_s.at[d + 1], zt_r.at[d + 1], z_down).start()
            else:
                hi = pl.ds(half, half)
                send(tok.at[d, x, hi], tok.at[d + 1, x, hi], zt_s.at[0], zt_r.at[0], z_down).start()
            tok_x(d)
            arrived(tok.at[e, x], zt_s.at[e], zt_r.at[e])
            if d < NZ // 2 - 1:
                send(tok.at[e, x], tok.at[e - 1, x], zt_s.at[e - 1], zt_r.at[e - 1], z_up).start()
            else:
                lo = pl.ds(0, half)
                send(tok.at[e, x, lo], tok.at[e - 1, x, lo], zt_s.at[e - 1], zt_r.at[e - 1], z_up).start()
            tok_x(e)
        else:
            arrived(tok.at[d, x, pl.ds(0, half)], zt_s.at[d], zt_r.at[d])
            arrived(tok.at[d, x, pl.ds(half, half)], zt_s.at[0], zt_r.at[0])
            tok_x(d)

    def og_start():
        for j in (2, 1, 3):
            send(og.at[0, x], og.at[0, x], ox_s.at[j - 1], ox_r.at[j - 1], x_peer[j]).start()

    def og_step(d):
        half = NX // 2
        if d == 0:
            for j in range(1, NX):
                arrived(og.at[0, 0], ox_s.at[j - 1], ox_r.at[j - 1])
            send(og.at[0], og.at[NZ - 1], oz_s.at[NZ - 1], oz_r.at[NZ - 1], z_up).start()
            send(og.at[0], og.at[1], oz_s.at[1], oz_r.at[1], z_down).start()
        elif d < NZ // 2:
            e = NZ - d
            arrived(og.at[d], oz_s.at[d], oz_r.at[d])
            if d < NZ // 2 - 1:
                send(og.at[d], og.at[d + 1], oz_s.at[d + 1], oz_r.at[d + 1], z_down).start()
            else:
                hi = pl.ds(half, half)
                send(og.at[d, hi], og.at[d + 1, hi], oz_s.at[0], oz_r.at[0], z_down).start()
            arrived(og.at[e], oz_s.at[e], oz_r.at[e])
            if d < NZ // 2 - 1:
                send(og.at[e], og.at[e - 1], oz_s.at[e - 1], oz_r.at[e - 1], z_up).start()
            else:
                lo = pl.ds(0, half)
                send(og.at[e, lo], og.at[e - 1, lo], oz_s.at[e - 1], oz_r.at[e - 1], z_up).start()
        else:
            arrived(og.at[d, pl.ds(0, half)], oz_s.at[d], oz_r.at[d])
            arrived(og.at[d, pl.ds(half, half)], oz_s.at[0], oz_r.at[0])

    def slot(p):
        return jnp.where(p % 2 == 1, (p + 1) // 2, (NZ - p // 2) % NZ)

    def s1(p):
        r = slot(p)
        for j in range(1, NX):
            arrived(tok.at[r, 0], xt_s.at[r, j - 1], xt_r.at[r, j - 1])
        a = tok[r].reshape(CHUNK, tokens.shape[1])

        @pl.loop(0, w.shape[1] // 256)
        def _(n):
            cols = pl.ds(pl.multiple_of(n * 256, 256), 256)
            part[r, :, :, :, cols] = jnp.dot(a, w[:, cols], preferred_element_type=F32).reshape(2, NY, PART, 256)

        send(part.at[r, 1 - c], core_in.at[r], c1_s.at[r], c1_r.at[r], sibling).start()

    def s2(p):
        r = slot(p)
        arrived(core_in.at[r], c1_s.at[r], c1_r.at[r])
        for j in (2, 1, 3):
            to = (y + j) % NY
            y_out[r, j - 1] = (part[r, c, to] + core_in[r, to]).astype(BF16)
            send(y_out.at[r, j - 1], y_in.at[r, j - 1], y1_s.at[r, j - 1], y1_r.at[r, j - 1], y_peer[j]).start()

    def s3(p):
        r = slot(p)
        total = part[r, c, y] + core_in[r, y]
        for j in (1, 3, 2):
            arrived(y_in.at[r, j - 1], y1_s.at[r, j - 1], y1_r.at[r, j - 1])
            total = total + y_in[r, j - 1].astype(F32)
        gate, up = total[:, :ff], total[:, ff:]
        hid[r, c * NY + y] = (gate / (1.0 + jnp.exp(-gate)) * up).astype(BF16)
        mine = hid.at[r, c * NY + y]
        for j in (2, 1, 3):
            send(mine, mine, y2_s.at[r, j - 1], y2_r.at[r, j - 1], y_peer[j]).start()

    def s4(p):
        r = slot(p)
        for j in (1, 3, 2):
            arrived(hid.at[r, 0], y2_s.at[r, j - 1], y2_r.at[r, j - 1])
        mine = hid.at[r, pl.ds(c * NY, NY)]
        send(mine, mine, c2_s.at[r], c2_r.at[r], sibling).start()

    def s5(p):
        r = slot(p)
        arrived(hid.at[r, pl.ds(0, NY)], c2_s.at[r], c2_r.at[r])
        h = hid[r].reshape(CHUNK, ff)

        @pl.loop(0, wd.shape[1] // 256)
        def _(n):
            cols = pl.ds(pl.multiple_of(n * 256, 256), 256)
            out = jnp.dot(h, wd[:, cols], preferred_element_type=F32).reshape(NX, OWN, 256)
            x_own[r, :, :, cols] = out
            x_out[r, :, :, cols] = out.astype(BF16)

        for j in (2, 1, 3):
            send(x_out.at[r, (x + j) % NX], x_in.at[r, j - 1], x2_s.at[r, j - 1], x2_r.at[r, j - 1], x_peer[j]).start()
        hid_t[:, pl.ds(pl.multiple_of(r * CHUNK, CHUNK), CHUNK)] = h.T

    def s6(p):
        r = slot(p)
        total = x_own[r, x]
        for j in (1, 3, 2):
            arrived(x_in.at[r, j - 1], x2_s.at[r, j - 1], x2_r.at[r, j - 1])
            total = total + x_in[r, j - 1].astype(F32)

        @pl.when(r == 0)
        def _():
            x_own[0, x] = total

        @pl.when(r != 0)
        def _():
            z_out[r] = total.astype(BF16)
            send(z_out.at[r], z_in.at[r], z2_s.at[r], z2_r.at[r], dev(x, y, (z + r) % NZ, c)).start()

    def grad(n):
        cols = pl.ds(n * 256, 256)
        dg[:, cols] = jnp.dot(
            hid_t[...], og[:, :, :, cols].reshape(NZ * CHUNK, 256), preferred_element_type=F32)
        pltpu.make_async_copy(dg.at[:, cols], down_grad.at[:, cols], dg_sem.at[n]).start()

    tok_step(0)

    @pl.loop(0, 11)
    def _(t):
        for d in range(1, NZ // 2 + 1):
            @pl.when(t == d - 1)
            def _():
                if d == 1:
                    loads[0].wait()
                    loads[1].wait()
                if d == 3:
                    loads[2].wait()
                tok_step(d)
                if d == 2:
                    og_start()

        @pl.when(t < NZ)
        def _():
            s1(t)

        @pl.when((t >= 3) & (t < NZ + 3))
        def _():
            s4(t - 3)

        @pl.when((t >= 2) & (t < NZ + 2))
        def _():
            s3(t - 2)

        @pl.when(t >= 6)
        def _():
            s6(t - 6)

        @pl.when((t >= 3) & (t < NZ + 3))
        def _():
            s5(t - 3)

        @pl.when(t < NZ)
        def _():
            s2(t)

        for d, at in enumerate((2, 4, 6, 8, 10)):
            @pl.when(t == at)
            def _():
                og_step(d)

    s6(jnp.int32(5))
    grad(0)
    grad(1)
    s6(jnp.int32(6))
    grad(2)
    grad(3)
    s6(jnp.int32(7))

    total = x_own[0, x]
    for r in (4, 3, 5, 2, 6, 1, 7):
        arrived(z_in.at[r], z2_s.at[r], z2_r.at[r])
        total = total + z_in[r].astype(F32)
    mixed[...] = total.astype(BF16)

    half = OWN // 2
    for r in range(NZ):
        if r in (0, NZ // 2):
            sent(tok.at[0, 0, pl.ds(0, half)], zt_s.at[r], zt_r.at[r])
            sent(og.at[0, pl.ds(0, NX // 2)], oz_s.at[r], oz_r.at[r])
        else:
            sent(tok.at[0, 0], zt_s.at[r], zt_r.at[r])
            sent(og.at[0], oz_s.at[r], oz_r.at[r])

    for j in range(NX - 1):
        sent(og.at[0, 0], ox_s.at[j], ox_r.at[j])

    @pl.loop(0, NZ)
    def _(r):
        sent(part.at[0, 0], c1_s.at[r], c1_r.at[r])
        sent(hid.at[0, pl.ds(0, NY)], c2_s.at[r], c2_r.at[r])
        for j in range(NX - 1):
            sent(tok.at[0, 0], xt_s.at[r, j], xt_r.at[r, j])
            sent(x_out.at[0, 0], x2_s.at[r, j], x2_r.at[r, j])
        for j in range(NY - 1):
            sent(y_out.at[0, 0], y1_s.at[r, j], y1_r.at[r, j])
            sent(hid.at[0, 0], y2_s.at[r, j], y2_r.at[r, j])

        @pl.when(r != 0)
        def _():
            sent(z_out.at[0], z2_s.at[r], z2_r.at[r])

    for n in range(dg.shape[1] // 256):
        cols = pl.ds(n * 256, 256)
        pltpu.make_async_copy(dg.at[:, cols], down_grad.at[:, cols], dg_sem.at[n]).wait()


def local(tokens, gate_w, up_w, down_w, out_grad):
    d, ff = gate_w.shape
    dma = pltpu.SemaphoreType.DMA
    vmem, hbm = pl.BlockSpec(memory_space=pltpu.VMEM), pl.BlockSpec(memory_space=pl.ANY)
    pair = lambda *shape: [dma(shape), dma(shape)]
    return pl.pallas_call(
        kernel,
        out_shape=(
            jax.ShapeDtypeStruct((OWN, d), BF16),
            jax.ShapeDtypeStruct((ff, d), F32),
        ),
        in_specs=[vmem, hbm, hbm, hbm, vmem],
        out_specs=(vmem, hbm),
        scratch_shapes=[
            pltpu.VMEM((d, 2 * ff), BF16),
            pltpu.VMEM((ff, d), BF16),
            pltpu.VMEM((NZ, NX, OWN, d), BF16),
            pltpu.VMEM((NZ, NX, OWN, d), BF16),
            pltpu.VMEM((NZ, 2, NY, PART, 2 * ff), F32),
            pltpu.VMEM((NZ, NY, PART, 2 * ff), F32),
            pltpu.VMEM((NZ, NY - 1, PART, 2 * ff), BF16),
            pltpu.VMEM((NZ, NY - 1, PART, 2 * ff), BF16),
            pltpu.VMEM((NZ, 2 * NY, PART, ff), BF16),
            pltpu.VMEM((ff, NZ * CHUNK), BF16),
            pltpu.VMEM((NZ, NX, OWN, d), F32),
            pltpu.VMEM((NZ, NX, OWN, d), BF16),
            pltpu.VMEM((NZ, NX - 1, OWN, d), BF16),
            pltpu.VMEM((NZ, OWN, d), BF16),
            pltpu.VMEM((NZ, OWN, d), BF16),
            pltpu.VMEM((ff, d), F32),
            dma((3,)),
            dma((d // 256,)),
            *pair(NZ), *pair(NZ, NX - 1), *pair(NZ), *pair(NZ, NY - 1), *pair(NZ, NY - 1),
            *pair(NZ), *pair(NZ, NX - 1), *pair(NZ), *pair(NX - 1), *pair(NZ),
        ],
        compiler_params=pltpu.CompilerParams(
            collective_id=0, has_side_effects=True, vmem_limit_bytes=56 * 2**20),
        cost_estimate=pl.CostEstimate(flops=7_600_000_000, bytes_accessed=10_000_000, transcendentals=120_000),
    )(tokens, gate_w, up_w, down_w, out_grad)


def solution(mesh):
    return jax.shard_map(
        local,
        mesh=mesh,
        in_specs=(P("col", "row"), P("row", "col"), P("row", "col"), P("col", "row"), P("col", "row")),
        out_specs=(P("col", "row"), P("col", "row")),
        check_vma=False,
    )
```

time: 509 us -> 86.4 us (0.17)
  waiting for transfers between devices: 463 us -> 0 us
  Pallas kernels: 0 us -> 79.7 us
  matrix products: 17 us -> 0 us
  between operations: 13.8 us -> 0.64 us
  other arithmetic: 9.59 us -> 0 us
    reduce_scatter x1 -> x0, waiting for transfers between devices: 215 us -> none  [local(): lax.psum_scatter(jnp.dot(block, down_weight, preferred_element_type=jnp.f...]
    all_gather x2 -> x0, waiting for transfers between devices: 147 us -> none  [the longest x1 80.5 us: local(): piece = lax.all_gather(tokens, 'col', axis=0, tiled=True)]
    psum x1 -> x0, waiting for transfers between devices: 99.3 us -> none  [local(): summed = lax.psum(partial_sums, 'row')]
    pallas_call x0 -> x1, Pallas kernels: none -> 79.7 us  [local(): pl.pallas_call(kernel, out_shape=(jax.ShapeDtypeStruct((OWN, d), BF16), j...]
    dot_general x4 -> x0, matrix products: 17 us -> none  [the longest x1 6.04 us: local(): lax.dot_general(block, lax.all_gather(out_grad, 'col', axis=0, tiled=True...]
    convert_element_type x2 -> x0, other arithmetic: 5.87 us -> none  [the longest x1 4.33 us: local(): (jax.nn.silu(summed[:, :hidden_width]) * summed[:, hidden_width:]).astype...]
  transfers between devices with their start and end apart: 4 -> 0, of which waited for: 4 -> 0; matrix products, arithmetic and copies ran while one was open for 3% -> 0% of each run, Pallas kernels for 0% -> 0%
where the time goes in v1:
time: 86.4 us; the launch traced here: 86.2 us
  Pallas kernels  79.7 us (92%)
  local copies, waits for them, and re-layouts  5.85 us (7%)
    pallas_call x1, Pallas kernels, local(): pl.pallas_call(kernel, out_shape=(jax.ShapeDtypeStruct((OWN, d), BF16), j...  79.7 us
    unnamed x2, local copies, waits for them, and re-layouts  5.85 us

profile of v1, /device:TPU:1, one launch (start us, length us, event | category | flops | bytes accessed | tf_op | source)
XLA Modules:
  0.0 86.2 jit_solution(9151795255280386670)
XLA Ops:
  0.6 79.7 %shard_map.68 = (bf16[32,1024]{1,0:T(8,128)(2,1)}, f32[896,1024]{1,0:T(8,128)}) custom-call(bf16[32,1024]{1,0:T(8,128)(2,1)} %tokens.1, bf16[1024,896]{1,0:T(8,128)(2,1)} %gate_w.1, bf16[1024,896]{1,0:T(8,128)(2,1)} %up_w.1, bf16[896,1024]{1,0:T(8,128)(2,1)} %down_w.1, bf16[32,1024]{1,0:T(8,128)(2,1)} %out_grad.1), custom_call_target="tpu_custom_call" | custom-call | flops 7600000000 | bytes 10000000 | tf_op jit(solution)/shard_map/pallas_call | solution.py:301
  80.3 1.5 %copy.9 = bf16[32,1024]{1,0:T(8,128)(2,1)} copy(bf16[32,1024]{1,0:T(8,128)(2,1)} %get-tuple-element.4) | data formatting | bytes 131072
  81.8 4.4 %copy.10 = f32[896,1024]{1,0:T(8,128)} copy(f32[896,1024]{1,0:T(8,128)} %get-tuple-element.5) | data formatting | bytes 7340032

commit v2 on v0

v2 whole, which is shorter than its diff:
```python
import jax
import jax.numpy as jnp
from jax import lax
from jax.experimental import pallas as pl
from jax.experimental.pallas import tpu as pltpu
from jax.sharding import PartitionSpec as P

MESH = pl.DeviceIdType.MESH
BF16, F32 = jnp.bfloat16, jnp.float32
NX, NY, NZ = 4, 4, 8
OWN = 32
CHUNK = NX * OWN
PART = CHUNK // (2 * NY)


ORDER = (0, 4, 3, 5, 2, 6, 7, 1)
FAR_FIRST = (4, 3, 5, 2, 6, 1, 7)
CUT = None


def schedule():
    return (
        ("tokr", 0), ("og_start",), ("s1", 0), ("tokr", 4), ("s2", 0), ("og", 0), ("tokr", 3), ("tokr", 5),
        ("s1", 1), ("tokr", 2), ("tokr", 6), ("tokr", 1), ("tokr", 7), ("s3", 0), ("s2", 1), ("s1", 2), ("s4", 0),
        ("s2", 2), ("s1", 3), ("s5", 0), ("og", 1), ("s3", 1), ("s2", 3), ("s1", 4), ("s3", 2), ("s1", 5),
        ("s2", 4), ("s4", 1), ("s2", 5), ("s5", 1), ("s3", 3), ("s4", 2), ("og", 2), ("s1", 6), ("s5", 2),
        ("s3", 4), ("s1", 7), ("s2", 6), ("s6", 0), ("s3", 5), ("s2", 7), ("s4", 3), ("s6", 1), ("s5", 3),
        ("s4", 4), ("og", 3), ("s5", 4), ("s3", 6), ("s6", 2), ("s4", 5), ("s5", 5), ("s3", 7), ("s6", 3),
        ("s4", 6), ("og", 4), ("s5", 6), ("s6", 4), ("s4", 7), ("s5", 7), ("s6", 5), ("grad", 0), ("grad", 1),
        ("grad", 2), ("grad", 3), ("s6", 6), ("s6", 7), ("s7",),
    )


def kernel(
    tokens, gate_w, up_w, down_w, out_grad, mixed, down_grad,
    w, wd, tok, og, part, core_in, y_out, y_in, hid, hid_t, x_own, x_out, x_in, z_out, z_in,
    w_sem, *sem_refs,
):
    ff = gate_w.shape[1]
    row, col = lax.axis_index("row"), lax.axis_index("col")
    y, c, x, z = row // 2, row % 2, col // NZ, col % NZ

    def dev(px, py, pz, pc):
        return (py * 2 + pc, px * NZ + pz)

    x_peer = [dev((x + j) % NX, y, z, c) for j in range(NX)]
    y_peer = [dev(x, (y + j) % NY, z, c) for j in range(NY)]
    z_peer = [dev(x, y, (z + j) % NZ, c) for j in range(NZ)]
    z_up, z_down = z_peer[1], z_peer[NZ - 1]
    sibling = dev(x, y, z, 1 - c)

    sems = {name: sem_refs[2 * i:2 * i + 2] for i, name in enumerate(SEMS)}
    started, seen = {}, set()

    def copy(key, src, dst, to):
        (ss, rs), at = sems[key[0]], key[1:]
        return pltpu.make_async_remote_copy(
            src_ref=src, dst_ref=dst, send_sem=ss.at[at], recv_sem=rs.at[at], device_id=to, device_id_type=MESH)

    def send(key, src, dst, to):
        copy(key, src, dst, to).start()
        started[key] = (src, dst)

    def arrived(*key):
        dst = started[key][1]
        copy(key, dst, dst, sibling).wait_recv()
        seen.add(key)

    loads = [
        pltpu.make_async_copy(tokens, tok.at[0, x], w_sem.at[3]),
        pltpu.make_async_copy(out_grad, og.at[0, x], w_sem.at[4]),
        pltpu.make_async_copy(gate_w, w.at[:, pl.ds(0, ff)], w_sem.at[0]),
        pltpu.make_async_copy(up_w, w.at[:, pl.ds(ff, ff)], w_sem.at[1]),
        pltpu.make_async_copy(down_w, wd, w_sem.at[2]),
    ]
    for load in loads:
        load.start()

    barrier = pltpu.get_barrier_semaphore()
    peers = x_peer[1:] + y_peer[1:] + z_peer[1:] + [sibling]
    for peer in peers:
        pl.semaphore_signal(barrier, inc=1, device_id=peer, device_id_type=MESH)
    loads[0].wait()
    loads[1].wait()
    pl.semaphore_wait(barrier, len(peers))

    def op_tokr(r):
        if r == 0:
            for q in FAR_FIRST:
                send(("zt", q), tok.at[0, x], tok.at[q, x], z_peer[NZ - q])
        else:
            arrived("zt", r)
        for j in (2, 1, 3):
            send(("xt", r, j - 1), tok.at[r, x], tok.at[r, x], x_peer[j])

    def ring(name, buf, rows, r):
        full, last = NZ // 2 - 1, NZ // 2
        lo, hi = pl.ds(0, rows // 2), pl.ds(rows // 2, rows // 2)
        if r < full:
            send((name, r + 1), buf(r), buf(r + 1), z_down)
        if r == full:
            send((name, 0), buf(r, hi), buf(last, hi), z_down)
        if r == last + 1:
            send((name, last), buf(r, lo), buf(last, lo), z_up)
        if r == 0 or r > last + 1:
            send((name, (r - 1) % NZ), buf(r), buf((r - 1) % NZ), z_up)

    def og_at(r, blocks=None):
        return og.at[r] if blocks is None else og.at[r, blocks]

    def ring_arrived(name, r):
        arrived(name, r)
        if r == NZ // 2:
            arrived(name, 0)

    def op_og_start():
        for j in (2, 1, 3):
            send(("ox", j - 1), og.at[0, x], og.at[0, x], x_peer[j])

    def op_og(d):
        if d == 0:
            for j in range(1, NX):
                arrived("ox", j - 1)
        for r in {0: (0,), NZ // 2: (NZ // 2,)}.get(d, (d, NZ - d)):
            if d > 0:
                ring_arrived("oz", r)
            ring("oz", og_at, NX, r)

    def op_s1(p):
        r = ORDER[p]
        if p == 0:
            loads[2].wait()
            loads[3].wait()
        for j in range(1, NX):
            arrived("xt", r, j - 1)
        a = tok[r].reshape(CHUNK, tokens.shape[1])

        for n in range(w.shape[1] // 256):
            cols = pl.ds(n * 256, 256)
            part[r, :, :, :, cols] = jnp.dot(a, w[:, cols], preferred_element_type=F32).reshape(2, NY, PART, 256)

        send(("c1", r), part.at[r, 1 - c], core_in.at[r], sibling)

    def op_s2(p):
        r = ORDER[p]
        arrived("c1", r)
        for j in (2, 1, 3):
            to = (y + j) % NY
            y_out[r, j - 1] = (part[r, c, to] + core_in[r, to]).astype(BF16)
            send(("y1", r, j - 1), y_out.at[r, j - 1], y_in.at[r, j - 1], y_peer[j])

    def op_s3(p):
        r = ORDER[p]
        total = part[r, c, y] + core_in[r, y]
        for j in (1, 3, 2):
            arrived("y1", r, j - 1)
            total = total + y_in[r, j - 1].astype(F32)
        gate, up = total[:, :ff], total[:, ff:]
        hid[r, c * NY + y] = (gate / (1.0 + jnp.exp(-gate)) * up).astype(BF16)
        mine = hid.at[r, c * NY + y]
        for j in (2, 1, 3):
            send(("y2", r, j - 1), mine, mine, y_peer[j])

    def op_s4(p):
        r = ORDER[p]
        for j in (1, 3, 2):
            arrived("y2", r, j - 1)
        mine = hid.at[r, pl.ds(c * NY, NY)]
        send(("c2", r), mine, mine, sibling)

    def op_s5(p):
        r = ORDER[p]
        if p == 0:
            loads[4].wait()
        arrived("c2", r)
        h = hid[r].reshape(CHUNK, ff)

        for n in range(wd.shape[1] // 256):
            cols = pl.ds(n * 256, 256)
            out = jnp.dot(h, wd[:, cols], preferred_element_type=F32).reshape(NX, OWN, 256)
            x_own[r, :, :, cols] = out
            x_out[r, :, :, cols] = out.astype(BF16)

        for j in (2, 1, 3):
            send(("x2", r, j - 1), x_out.at[r, (x + j) % NX], x_in.at[r, j - 1], x_peer[j])
        hid_t[:, pl.ds(r * CHUNK, CHUNK)] = h.T

    def op_s6(p):
        r = ORDER[p]
        total = x_own[r, x]
        for j in (1, 3, 2):
            arrived("x2", r, j - 1)
            total = total + x_in[r, j - 1].astype(F32)
        if r == 0:
            x_own[0, x] = total
        else:
            z_out[r] = total.astype(BF16)
            send(("z2", r), z_out.at[r], z_in.at[r], z_peer[r])

    def op_grad(n):
        cols = pl.ds(n * 256, 256)
        down_grad[:, cols] = jnp.dot(
            hid_t[...], og[:, :, :, cols].reshape(NZ * CHUNK, 256), preferred_element_type=F32)

    def op_s7():
        total = x_own[0, x]
        for r in ORDER[1:]:
            arrived("z2", r)
            total = total + z_in[r].astype(F32)
        mixed[...] = total.astype(BF16)

    ops = {"tokr": op_tokr, "og_start": op_og_start, "og": op_og, "s1": op_s1, "s2": op_s2, "s3": op_s3, "s4": op_s4,
           "s5": op_s5, "s6": op_s6, "grad": op_grad, "s7": op_s7}
    for op in schedule()[:CUT]:
        ops[op[0]](*op[1:])
    if CUT is not None:
        for key in started:
            if key not in seen:
                arrived(*key)
        done = {op for op in schedule()[:CUT]}
        if ("s1", 0) not in done:
            loads[2].wait()
            loads[3].wait()
        if ("s5", 0) not in done:
            loads[4].wait()
    for key, (src, _) in started.items():
        copy(key, src, src, sibling).wait_send()


def finish(mixed, down_grad, mixed_out, down_grad_out, sem):
    copies = [
        pltpu.make_async_copy(mixed, mixed_out, sem.at[0]),
        pltpu.make_async_copy(down_grad, down_grad_out, sem.at[1]),
    ]
    for copy in copies:
        copy.start()
    for copy in copies:
        copy.wait()


SEMS = {
    "zt": (NZ,), "xt": (NZ, NX - 1), "c1": (NZ,), "y1": (NZ, NY - 1), "y2": (NZ, NY - 1),
    "c2": (NZ,), "x2": (NZ, NX - 1), "z2": (NZ,), "ox": (NX - 1,), "oz": (NZ,),
}


def local(tokens, gate_w, up_w, down_w, out_grad):
    d, ff = gate_w.shape
    dma = pltpu.SemaphoreType.DMA
    vmem, hbm = pl.BlockSpec(memory_space=pltpu.VMEM), pl.BlockSpec(memory_space=pltpu.HBM)
    mixed, down_grad = pl.pallas_call(
        kernel,
        out_shape=(
            pltpu.VMEM((OWN, d), BF16),
            pltpu.VMEM((ff, d), F32),
        ),
        in_specs=[hbm] * 5,
        out_specs=(vmem, vmem),
        scratch_shapes=[
            pltpu.VMEM((d, 2 * ff), BF16),
            pltpu.VMEM((ff, d), BF16),
            pltpu.VMEM((NZ, NX, OWN, d), BF16),
            pltpu.VMEM((NZ, NX, OWN, d), BF16),
            pltpu.VMEM((NZ, 2, NY, PART, 2 * ff), F32),
            pltpu.VMEM((NZ, NY, PART, 2 * ff), F32),
            pltpu.VMEM((NZ, NY - 1, PART, 2 * ff), BF16),
            pltpu.VMEM((NZ, NY - 1, PART, 2 * ff), BF16),
            pltpu.VMEM((NZ, 2 * NY, PART, ff), BF16),
            pltpu.VMEM((ff, NZ * CHUNK), BF16),
            pltpu.VMEM((NZ, NX, OWN, d), F32),
            pltpu.VMEM((NZ, NX, OWN, d), BF16),
            pltpu.VMEM((NZ, NX - 1, OWN, d), BF16),
            pltpu.VMEM((NZ, OWN, d), BF16),
            pltpu.VMEM((NZ, OWN, d), BF16),
            dma((5,)),
            *[dma(shape) for shape in SEMS.values() for _ in range(2)],
        ],
        compiler_params=pltpu.CompilerParams(
            collective_id=0, has_side_effects=True, vmem_limit_bytes=42 * 2**20),
        cost_estimate=pl.CostEstimate(flops=7_600_000_000, bytes_accessed=10_000_000, transcendentals=120_000),
    )(*[pltpu.with_memory_space_constraint(a, pltpu.HBM) for a in (tokens, gate_w, up_w, down_w, out_grad)])
    return pl.pallas_call(
        finish,
        out_shape=(
            jax.ShapeDtypeStruct((OWN, d), BF16),
            jax.ShapeDtypeStruct((ff, d), F32),
        ),
        in_specs=[vmem, vmem],
        out_specs=(hbm, hbm),
        scratch_shapes=[dma((2,))],
        compiler_params=pltpu.CompilerParams(vmem_limit_bytes=2**20),
    )(*[pltpu.with_memory_space_constraint(a, pltpu.VMEM) for a in (mixed, down_grad)])


def solution(mesh):
    return jax.shard_map(
        local,
        mesh=mesh,
        in_specs=(P("col", "row"), P("row", "col"), P("row", "col"), P("col", "row"), P("col", "row")),
        out_specs=(P("col", "row"), P("col", "row")),
        check_vma=False,
    )
```

time: 509 us -> 72.9 us (0.14)
  waiting for transfers between devices: 463 us -> 0 us
  Pallas kernels: 0 us -> 72.2 us
  matrix products: 17 us -> 0 us
  between operations: 13.8 us -> 0.64 us
  other arithmetic: 9.59 us -> 0 us
    reduce_scatter x1 -> x0, waiting for transfers between devices: 215 us -> none  [local(): lax.psum_scatter(jnp.dot(block, down_weight, preferred_element_type=jnp.f...]
    all_gather x2 -> x0, waiting for transfers between devices: 147 us -> none  [the longest x1 80.5 us: local(): piece = lax.all_gather(tokens, 'col', axis=0, tiled=True)]
    psum x1 -> x0, waiting for transfers between devices: 99.3 us -> none  [local(): summed = lax.psum(partial_sums, 'row')]
    pallas_call x0 -> x2, Pallas kernels: none -> 72.2 us  [the longest x1 70.3 us: local(): pl.pallas_call(kernel, out_shape=(pltpu.VMEM((OWN, d), BF16), pltpu.VMEM(...]
    dot_general x4 -> x0, matrix products: 17 us -> none  [the longest x1 6.04 us: local(): lax.dot_general(block, lax.all_gather(out_grad, 'col', axis=0, tiled=True...]
    convert_element_type x2 -> x0, other arithmetic: 5.87 us -> none  [the longest x1 4.33 us: local(): (jax.nn.silu(summed[:, :hidden_width]) * summed[:, hidden_width:]).astype...]
  transfers between devices with their start and end apart: 4 -> 0, of which waited for: 4 -> 0; matrix products, arithmetic and copies ran while one was open for 3% -> 0% of each run, Pallas kernels for 0% -> 0%
where the time goes in v2:
time: 72.9 us; the launch traced here: 72.8 us
  Pallas kernels  72.2 us (99%)
    pallas_call x1, Pallas kernels, local(): pl.pallas_call(kernel, out_shape=(pltpu.VMEM((OWN, d), BF16), pltpu.VMEM(...  70.3 us
    pallas_call x1, Pallas kernels, local(): pl.pallas_call(finish, out_shape=(jax.ShapeDtypeStruct((OWN, d), BF16), j...  1.88 us

profile of v2, /device:TPU:1, one launch (start us, length us, event | category | flops | bytes accessed | tf_op | source)
XLA Modules:
  0.0 72.8 jit_solution(2020449936369114307)
XLA Ops:
  0.6 70.3 %shard_map.68 = (bf16[32,1024]{1,0:T(8,128)(2,1)S(1)}, f32[896,1024]{1,0:T(8,128)S(1)}) custom-call(bf16[32,1024]{1,0:T(8,128)(2,1)} %tokens.1, bf16[1024,896]{1,0:T(8,128)(2,1)} %gate_w.1, bf16[1024,896]{1,0:T(8,128)(2,1)} %up_w.1, bf16[896,1024]{1,0:T(8,128)(2,1)} %down_w.1, bf16[32,1024]{1,0:T(8,128)(2,1)} %out_grad.1), custom_call_target="tpu_custom_call" | custom-call | flops 7600000000 | bytes 10000000 | tf_op jit(solution)/shard_map/pallas_call | solution.py:251
  71.0 1.9 %shard_map.69 = (bf16[32,1024]{1,0:T(8,128)(2,1)}, f32[896,1024]{1,0:T(8,128)}) custom-call(bf16[32,1024]{1,0:T(8,128)(2,1)S(1)} %get-tuple-element.4.mixed, f32[896,1024]{1,0:T(8,128)S(1)} %get-tuple-element.5.down_grad), custom_call_target="tpu_custom_call" | custom-call | tf_op jit(solution)/shard_map/pallas_call | solution.py:282

commit v3 on v2

--- a/solution.py
+++ b/solution.py
@@ -13,21 +13,19 @@
 PART = CHUNK // (2 * NY)
 
 
-ORDER = (0, 4, 3, 5, 2, 6, 7, 1)
-FAR_FIRST = (4, 3, 5, 2, 6, 1, 7)
-CUT = None
-
+ORDER = (0, 7, 2, 3, 1, 4, 5, 6)
 
 def schedule():
     return (
-        ("tokr", 0), ("og_start",), ("s1", 0), ("tokr", 4), ("s2", 0), ("og", 0), ("tokr", 3), ("tokr", 5),
-        ("s1", 1), ("tokr", 2), ("tokr", 6), ("tokr", 1), ("tokr", 7), ("s3", 0), ("s2", 1), ("s1", 2), ("s4", 0),
-        ("s2", 2), ("s1", 3), ("s5", 0), ("og", 1), ("s3", 1), ("s2", 3), ("s1", 4), ("s3", 2), ("s1", 5),
-        ("s2", 4), ("s4", 1), ("s2", 5), ("s5", 1), ("s3", 3), ("s4", 2), ("og", 2), ("s1", 6), ("s5", 2),
-        ("s3", 4), ("s1", 7), ("s2", 6), ("s6", 0), ("s3", 5), ("s2", 7), ("s4", 3), ("s6", 1), ("s5", 3),
-        ("s4", 4), ("og", 3), ("s5", 4), ("s3", 6), ("s6", 2), ("s4", 5), ("s5", 5), ("s3", 7), ("s6", 3),
-        ("s4", 6), ("og", 4), ("s5", 6), ("s6", 4), ("s4", 7), ("s5", 7), ("s6", 5), ("grad", 0), ("grad", 1),
-        ("grad", 2), ("grad", 3), ("s6", 6), ("s6", 7), ("s7",),
+        ("tokr", 0), ("zs", 2), ("zs", 7), ("zs", 5), ("og_start",), ("tokr", 7), ("zs", 4), ("s1", 0), ("zs", 3),
+        ("ogs", 0), ("tokr", 2), ("tokr", 5), ("zs", 6), ("s2", 0), ("s1", 1), ("s2", 1), ("s1", 2), ("tokr", 4),
+        ("zs", 1), ("s3", 0), ("s2", 2), ("ogs", 7), ("s1", 6), ("tokr", 3), ("s2", 6), ("s3", 1), ("tokr", 6),
+        ("ogs", 1), ("s4", 0), ("s1", 5), ("s5", 0), ("s3", 2), ("tokr", 1), ("s2", 5), ("ogs", 6), ("s1", 3),
+        ("s4", 1), ("s3", 6), ("s1", 7), ("s2", 3), ("s5", 1), ("ogs", 2), ("s4", 2), ("s3", 5), ("s5", 2),
+        ("s2", 7), ("s1", 4), ("s3", 3), ("s4", 6), ("s2", 4), ("s5", 6), ("s4", 5), ("s3", 7), ("s5", 5),
+        ("ogs", 3), ("s4", 3), ("ogs", 5), ("s6", 2), ("s5", 3), ("s3", 4), ("s4", 7), ("s6", 6), ("s5", 7),
+        ("s4", 4), ("s6", 5), ("ogs", 4), ("s6", 0), ("s6", 1), ("s5", 4), ("s6", 3), ("s6", 7), ("grad", 3),
+        ("s6", 4), ("grad", 1), ("grad", 2), ("grad", 0), ("s7",),
     )
 
 
@@ -50,7 +48,7 @@
     sibling = dev(x, y, z, 1 - c)
 
     sems = {name: sem_refs[2 * i:2 * i + 2] for i, name in enumerate(SEMS)}
-    started, seen = {}, set()
+    started = {}
 
     def copy(key, src, dst, to):
         (ss, rs), at = sems[key[0]], key[1:]
@@ -64,7 +62,6 @@
     def arrived(*key):
         dst = started[key][1]
         copy(key, dst, dst, sibling).wait_recv()
-        seen.add(key)
 
     loads = [
         pltpu.make_async_copy(tokens, tok.at[0, x], w_sem.at[3]),
@@ -84,11 +81,11 @@
     loads[1].wait()
     pl.semaphore_wait(barrier, len(peers))
 
+    def op_zs(r):
+        send(("zt", r), tok.at[0, x], tok.at[r, x], z_peer[NZ - r])
+
     def op_tokr(r):
-        if r == 0:
-            for q in FAR_FIRST:
-                send(("zt", q), tok.at[0, x], tok.at[q, x], z_peer[NZ - q])
-        else:
+        if r > 0:
             arrived("zt", r)
         for j in (2, 1, 3):
             send(("xt", r, j - 1), tok.at[r, x], tok.at[r, x], x_peer[j])
@@ -117,14 +114,13 @@
         for j in (2, 1, 3):
             send(("ox", j - 1), og.at[0, x], og.at[0, x], x_peer[j])
 
-    def op_og(d):
-        if d == 0:
+    def op_ogs(r):
+        if r == 0:
             for j in range(1, NX):
                 arrived("ox", j - 1)
-        for r in {0: (0,), NZ // 2: (NZ // 2,)}.get(d, (d, NZ - d)):
-            if d > 0:
-                ring_arrived("oz", r)
-            ring("oz", og_at, NX, r)
+        else:
+            ring_arrived("oz", r)
+        ring("oz", og_at, NX, r)
 
     def op_s1(p):
         r = ORDER[p]
@@ -209,20 +205,10 @@
             total = total + z_in[r].astype(F32)
         mixed[...] = total.astype(BF16)
 
-    ops = {"tokr": op_tokr, "og_start": op_og_start, "og": op_og, "s1": op_s1, "s2": op_s2, "s3": op_s3, "s4": op_s4,
+    ops = {"zs": op_zs, "tokr": op_tokr, "og_start": op_og_start, "ogs": op_ogs, "s1": op_s1, "s2": op_s2, "s3": op_s3, "s4": op_s4,
            "s5": op_s5, "s6": op_s6, "grad": op_grad, "s7": op_s7}
-    for op in schedule()[:CUT]:
+    for op in schedule():
         ops[op[0]](*op[1:])
-    if CUT is not None:
-        for key in started:
-            if key not in seen:
-                arrived(*key)
-        done = {op for op in schedule()[:CUT]}
-        if ("s1", 0) not in done:
-            loads[2].wait()
-            loads[3].wait()
-        if ("s5", 0) not in done:
-            loads[4].wait()
     for key, (src, _) in started.items():
         copy(key, src, src, sibling).wait_send()
 

time: 72.9 us -> 70.9 us (0.973)
  Pallas kernels: 72.2 us -> 70.2 us
    pallas_call x1, Pallas kernels: 70.3 us -> 68.3 us  [local(): pl.pallas_call(kernel, out_shape=(pltpu.VMEM((OWN, d), BF16), pltpu.VMEM(...]
where the time goes in v3:
time: 70.9 us; the launch traced here: 70.8 us
  Pallas kernels  70.2 us (99%)
    pallas_call x1, Pallas kernels, local(): pl.pallas_call(kernel, out_shape=(pltpu.VMEM((OWN, d), BF16), pltpu.VMEM(...  68.3 us
    pallas_call x1, Pallas kernels, local(): pl.pallas_call(finish, out_shape=(jax.ShapeDtypeStruct((OWN, d), BF16), j...  1.88 us

profile of v3, /device:TPU:1, one launch (start us, length us, event | category | flops | bytes accessed | tf_op | source)
XLA Modules:
  0.0 70.8 jit_solution(6881151464852499256)
XLA Ops:
  0.6 68.3 %shard_map.68 = (bf16[32,1024]{1,0:T(8,128)(2,1)S(1)}, f32[896,1024]{1,0:T(8,128)S(1)}) custom-call(bf16[32,1024]{1,0:T(8,128)(2,1)} %tokens.1, bf16[1024,896]{1,0:T(8,128)(2,1)} %gate_w.1, bf16[1024,896]{1,0:T(8,128)(2,1)} %up_w.1, bf16[896,1024]{1,0:T(8,128)(2,1)} %down_w.1, bf16[32,1024]{1,0:T(8,128)(2,1)} %out_grad.1), custom_call_target="tpu_custom_call" | custom-call | flops 7600000000 | bytes 10000000 | tf_op jit(solution)/shard_map/pallas_call | solution.py:237
  68.9 1.9 %shard_map.69 = (bf16[32,1024]{1,0:T(8,128)(2,1)}, f32[896,1024]{1,0:T(8,128)}) custom-call(bf16[32,1024]{1,0:T(8,128)(2,1)S(1)} %get-tuple-element.4.mixed, f32[896,1024]{1,0:T(8,128)S(1)} %get-tuple-element.5.down_grad), custom_call_target="tpu_custom_call" | custom-call | tf_op jit(solution)/shard_map/pallas_call | solution.py:268

commit v4 on v3

--- a/solution.py
+++ b/solution.py
@@ -14,6 +14,7 @@
 
 
 ORDER = (0, 7, 2, 3, 1, 4, 5, 6)
+
 
 def schedule():
     return (
@@ -199,6 +200,8 @@
             hid_t[...], og[:, :, :, cols].reshape(NZ * CHUNK, 256), preferred_element_type=F32)
 
     def op_s7():
+        for key, (src, _) in started.items():
+            copy(key, src, src, sibling).wait_send()
         total = x_own[0, x]
         for r in ORDER[1:]:
             arrived("z2", r)
@@ -209,8 +212,6 @@
            "s5": op_s5, "s6": op_s6, "grad": op_grad, "s7": op_s7}
     for op in schedule():
         ops[op[0]](*op[1:])
-    for key, (src, _) in started.items():
-        copy(key, src, src, sibling).wait_send()
 
 
 def finish(mixed, down_grad, mixed_out, down_grad_out, sem):

time: 70.9 us -> 70.7 us (level)
  no operation moved by 1% of the time
where the time goes in v4:
time: 70.7 us; the launch traced here: 70.6 us
  Pallas kernels  70 us (99%)
    pallas_call x1, Pallas kernels, local(): pl.pallas_call(kernel, out_shape=(pltpu.VMEM((OWN, d), BF16), pltpu.VMEM(...  68.1 us
    pallas_call x1, Pallas kernels, local(): pl.pallas_call(finish, out_shape=(jax.ShapeDtypeStruct((OWN, d), BF16), j...  1.88 us

profile of v4, /device:TPU:1, one launch (start us, length us, event | category | flops | bytes accessed | tf_op | source)
XLA Modules:
  0.0 70.6 jit_solution(16720549070289851185)
XLA Ops:
  0.6 68.1 %shard_map.68 = (bf16[32,1024]{1,0:T(8,128)(2,1)S(1)}, f32[896,1024]{1,0:T(8,128)S(1)}) custom-call(bf16[32,1024]{1,0:T(8,128)(2,1)} %tokens.1, bf16[1024,896]{1,0:T(8,128)(2,1)} %gate_w.1, bf16[1024,896]{1,0:T(8,128)(2,1)} %up_w.1, bf16[896,1024]{1,0:T(8,128)(2,1)} %down_w.1, bf16[32,1024]{1,0:T(8,128)(2,1)} %out_grad.1), custom_call_target="tpu_custom_call" | custom-call | flops 7600000000 | bytes 10000000 | tf_op jit(solution)/shard_map/pallas_call | solution.py:238
  68.7 1.9 %shard_map.69 = (bf16[32,1024]{1,0:T(8,128)(2,1)}, f32[896,1024]{1,0:T(8,128)}) custom-call(bf16[32,1024]{1,0:T(8,128)(2,1)S(1)} %get-tuple-element.4.mixed, f32[896,1024]{1,0:T(8,128)S(1)} %get-tuple-element.5.down_grad), custom_call_target="tpu_custom_call" | custom-call | tf_op jit(solution)/shard_map/pallas_call | solution.py:269

commit v5 on v4

--- a/solution.py
+++ b/solution.py
@@ -75,7 +75,8 @@
         load.start()
 
     barrier = pltpu.get_barrier_semaphore()
-    peers = x_peer[1:] + y_peer[1:] + z_peer[1:] + [sibling]
+    peers = [z_peer[j] for j in (4, 3, 5, 2, 6)] + [x_peer[2], y_peer[2]]
+    peers += [z_up, z_down, x_peer[1], x_peer[3], y_peer[1], y_peer[3], sibling]
     for peer in peers:
         pl.semaphore_signal(barrier, inc=1, device_id=peer, device_id_type=MESH)
     loads[0].wait()
@@ -135,12 +136,14 @@
         for n in range(w.shape[1] // 256):
             cols = pl.ds(n * 256, 256)
             part[r, :, :, :, cols] = jnp.dot(a, w[:, cols], preferred_element_type=F32).reshape(2, NY, PART, 256)
-
-        send(("c1", r), part.at[r, 1 - c], core_in.at[r], sibling)
+            if n == 3 or n == w.shape[1] // 256 - 1:
+                go = pl.ds(0, 1024) if n == 3 else pl.ds(1024, w.shape[1] - 1024)
+                send(("c1", r, n // 4), part.at[r, 1 - c, :, :, go], core_in.at[r, :, :, go], sibling)
 
     def op_s2(p):
         r = ORDER[p]
-        arrived("c1", r)
+        arrived("c1", r, 0)
+        arrived("c1", r, 1)
         for j in (2, 1, 3):
             to = (y + j) % NY
             y_out[r, j - 1] = (part[r, c, to] + core_in[r, to]).astype(BF16)
@@ -226,7 +229,7 @@
 
 
 SEMS = {
-    "zt": (NZ,), "xt": (NZ, NX - 1), "c1": (NZ,), "y1": (NZ, NY - 1), "y2": (NZ, NY - 1),
+    "zt": (NZ,), "xt": (NZ, NX - 1), "c1": (NZ, 2), "y1": (NZ, NY - 1), "y2": (NZ, NY - 1),
     "c2": (NZ,), "x2": (NZ, NX - 1), "z2": (NZ,), "ox": (NX - 1,), "oz": (NZ,),
 }
 

time: 70.7 us -> 70.8 us (level)
  no operation moved by 1% of the time
where the time goes in v5:
time: 70.8 us; the launch traced here: 70.7 us
  Pallas kernels  70.1 us (99%)
    pallas_call x1, Pallas kernels, local(): pl.pallas_call(kernel, out_shape=(pltpu.VMEM((OWN, d), BF16), pltpu.VMEM(...  68.2 us
    pallas_call x1, Pallas kernels, local(): pl.pallas_call(finish, out_shape=(jax.ShapeDtypeStruct((OWN, d), BF16), j...  1.88 us

profile of v5, /device:TPU:1, one launch (start us, length us, event | category | flops | bytes accessed | tf_op | source)
XLA Modules:
  0.0 70.7 jit_solution(4039021444422452343)
XLA Ops:
  0.6 68.2 %shard_map.68 = (bf16[32,1024]{1,0:T(8,128)(2,1)S(1)}, f32[896,1024]{1,0:T(8,128)S(1)}) custom-call(bf16[32,1024]{1,0:T(8,128)(2,1)} %tokens.1, bf16[1024,896]{1,0:T(8,128)(2,1)} %gate_w.1, bf16[1024,896]{1,0:T(8,128)(2,1)} %up_w.1, bf16[896,1024]{1,0:T(8,128)(2,1)} %down_w.1, bf16[32,1024]{1,0:T(8,128)(2,1)} %out_grad.1), custom_call_target="tpu_custom_call" | custom-call | flops 7600000000 | bytes 10000000 | tf_op jit(solution)/shard_map/pallas_call | solution.py:241
  68.8 1.9 %shard_map.69 = (bf16[32,1024]{1,0:T(8,128)(2,1)}, f32[896,1024]{1,0:T(8,128)}) custom-call(bf16[32,1024]{1,0:T(8,128)(2,1)S(1)} %get-tuple-element.4.mixed, f32[896,1024]{1,0:T(8,128)S(1)} %get-tuple-element.5.down_grad), custom_call_target="tpu_custom_call" | custom-call | tf_op jit(solution)/shard_map/pallas_call | solution.py:272
